TPU v7x, 512 devices: a whole 4x4x16 slice. The times are simulated.
512 devices in a mesh: row: 16 (over z_hi, x, core), col: 32 (over y, z_lo).
Axes of the slice: x: 4, y: 4, z: 16 (z_hi: 2, z_lo: 8; z = z_hi * 8 + z_lo), core: 2. Of those that a mesh axis runs over, the one named last changes fastest.
Arguments:
- adjoint: bfloat16 [16, 16, 32, 8, 128, 128], P('row', None, 'col'), may hold values from -0.26367188 to 0.26367188
- features: float32 [32768, 32], P('row'), may hold values from -1.5 to 1.5
- tile_of_slot: int32 [256], replicated, may hold values from 0 to 255, each once
Outputs:
- features_grad: float32 [32768, 32], P('row')
Inputs may be any that keep to these rules, and one draw needn't show every extreme that they name: `tile_of_slot`: each tile number appears in exactly one slot.
All inputs are finite; a program needn't handle non-finite values.
Results may differ from a plain program's by a relative error of at most 0.0003.
Values sent between devices are 32-bit elements; how exact they have to be, the bound alone decides.
A program may use at most 64 MiB of HBM per device.

v0:
```python
import jax
import jax.numpy as jnp
from jax import lax
from jax.sharding import PartitionSpec as P


def broadcast(value, axis, source):
    kept = jnp.where(lax.axis_index(axis) == source, value, 0).astype(value.dtype)
    return lax.psum(kept, axis)


def per_device(adjoint, features, tile_of_slot):
    hi = lax.Precision.HIGHEST
    nrow = lax.axis_size("row")
    ncol = lax.axis_size("col")
    rindex = lax.axis_index("row")
    cindex = lax.axis_index("col")
    nrt = adjoint.shape[1]
    nct = adjoint.shape[3]
    bsize = adjoint.shape[-1]
    width = features.shape[-1]
    mgroup = nrt // nrow
    repeat = ncol // nrow
    ntiles = tile_of_slot.shape[0]
    local = features.reshape(mgroup, nrow, bsize, width)
    row_feats = lax.all_to_all(local, "row", split_axis=1, concat_axis=0, tiled=True).reshape(
        nrt, bsize, width
    )
    picks = row_feats.reshape(nct, repeat, bsize, width)
    chosen = lax.dynamic_index_in_dim(picks, cindex // nrow, 1, False)
    col_feats = broadcast(chosen, "row", cindex % nrow)
    row_slots = jnp.arange(nrt, dtype=jnp.int32) * nrow + rindex
    col_slots = jnp.arange(nct, dtype=jnp.int32) * ncol + cindex
    every = jnp.arange(ntiles, dtype=jnp.int32)
    row_tile = jnp.sum(
        jnp.where(every[None, :] == row_slots[:, None], tile_of_slot[None, :], 0), axis=1
    )
    col_tile = jnp.sum(
        jnp.where(every[None, :] == col_slots[:, None], tile_of_slot[None, :], 0), axis=1
    )
    lower = jnp.arange(bsize)[:, None] >= jnp.arange(bsize)[None, :]
    col_sq = jnp.sum(col_feats * col_feats, axis=-1)
    tiles_local = adjoint.reshape(nrt, nct, bsize, bsize)

    def step(carry, inputs):
        tiles, frow, rtile, rslot = inputs
        dist = (
            jnp.sum(frow * frow, axis=-1)[None, :, None]
            + col_sq[:, None, :]
            - 2.0 * jnp.einsum("if,cjf->cij", frow, col_feats, precision=hi)
        )
        kern = jnp.exp(-0.25 * dist)
        live = rtile > col_tile
        diag = (col_slots == rslot)[:, None, None] & lower[None]
        mask = jnp.where(live[:, None, None] | diag, 1.0, 0.0).astype(jnp.float32)
        weight = tiles.astype(jnp.float32) * kern * mask
        rowpart = jnp.sum(weight, axis=(0, 2))[:, None] * frow - jnp.einsum(
            "cij,cjf->if", weight, col_feats, precision=hi
        )
        colpart = jnp.sum(weight, axis=1)[..., None] * col_feats - jnp.einsum(
            "cij,if->cjf", weight, frow, precision=hi
        )
        return (carry + colpart, rowpart)

    col_part, row_part = lax.scan(
        step,
        jnp.zeros((nct, bsize, width), jnp.float32),
        (tiles_local, row_feats, row_tile, row_slots),
    )
    col_total = lax.psum(col_part, "row")
    owner = rindex == cindex % nrow
    place = (jnp.arange(repeat) == cindex // nrow)[None, :, None, None] & owner
    embedded = jnp.where(place, col_total[:, None], 0.0).reshape(nrt, bsize, width)
    total = row_part + embedded
    summed = lax.psum(total, "col")
    sectioned = summed.reshape(nrow, mgroup, 1, bsize, width)
    back = lax.all_to_all(sectioned, "row", split_axis=0, concat_axis=2, tiled=True)
    result = back.reshape(nrt * bsize, width)
    return -0.5 * result


def solution(mesh):
    return jax.shard_map(
        per_device,
        mesh=mesh,
        in_specs=(P("row", None, "col", None, None, None), P("row", None), P()),
        out_specs=P("row", None),
        check_vma=False,
    )
```

profile of v0, /device:TPU:6, one launch (start us, length us, event | category | flops | bytes accessed | tf_op | source)
XLA Modules:
  0.0 1161.5 jit_solution(8959670831249913361)
XLA Ops:
  8.3 18.0 %all-to-all-start = ((f32[1,16,128,32]{2,3,0,1:T(8,128)}), f32[1,16,128,32]{2,3,0,1:T(8,128)S(1)}, u32[]{:S(2)}, u32[]{:S(2)}) async-start(f32[1,16,128,32]{2,3,0,1:T(8,128)} %copy.11), calls=%async_computation | async-start | bytes 524288 | tf_op jit(solution)/shard_map/all_to_all | solution.py:26
  27.3 14.4 %all-to-all-done = f32[1,16,128,32]{2,3,0,1:T(8,128)S(1)} async-done(((f32[1,16,128,32]{2,3,0,1:T(8,128)}), f32[1,16,128,32]{2,3,0,1:T(8,128)S(1)}, u32[]{:S(2)}, u32[]{:S(2)}) %all-to-all-start) | async-done | bytes 262176 | tf_op jit(solution)/shard_map/all_to_all | solution.py:26
  43.3 251.7 %all-reduce.4.cloned.1.call-done = f32[8,128,32]{1,2,0:T(8,128)} async-done(((f32[8,128,32]{1,2,0:T(8,128)}), f32[8,128,32]{1,2,0:T(8,128)}) %all-reduce.4.cloned.1.call-update) | async-done | bytes 131088 | tf_op jit(solution)/shard_map/psum | solution.py:9
  296.0 117.8 %while.14 = (s32[]{:T(128)}, f32[8,128,32]{1,2,0:T(8,128)S(1)}, f32[16,128,32]{1,2,0:T(8,128)S(1)}, bf16[16,8,128,128]{3,2,1,0:T(8,128)(2,1)}, f32[16,128,32]{1,...) while((s32[]{:T(128)}, f32[8,128,32]{1,2,0:T(8,128)S(1)}, ...), condition=%wide.region_8.9_spmd.clone.clone, body=%wide.region_4.8_spmd.clone.sunk.clone | while | flops 152730400 | bytes 2621663 | solution.py:65
  298.5 2.0 fusion.51
  301.8 1.5 fusion.53
  305.9 2.0 fusion.51
  307.9 1.3 fusion.52
  309.2 1.5 fusion.53
  313.3 2.0 fusion.51
  316.6 1.5 fusion.53
  320.6 2.0 fusion.51
  322.6 1.3 fusion.52
  323.9 1.5 fusion.53
  328.0 2.0 fusion.51
  330.0 1.3 fusion.52
  331.3 1.5 fusion.53
  335.4 2.0 fusion.51
  337.3 1.3 fusion.52
  338.6 1.5 fusion.53
  342.7 2.0 fusion.51
  344.7 1.3 fusion.52
  346.0 1.5 fusion.53
  350.1 2.0 fusion.51
  352.0 1.3 fusion.52
  353.4 1.5 fusion.53
  357.5 2.0 fusion.51
  359.4 1.3 fusion.52
  360.7 1.5 fusion.53
  364.8 2.0 fusion.51
  366.8 1.3 fusion.52
  368.1 1.5 fusion.53
  372.2 2.0 fusion.51
  375.5 1.5 fusion.53
  379.5 2.0 fusion.51
  382.8 1.5 fusion.53
  386.9 2.0 fusion.51
  390.2 1.5 fusion.53
  394.3 2.0 fusion.51
  397.6 1.5 fusion.53
  401.6 2.0 fusion.51
  404.9 1.5 fusion.53
  409.0 2.0 fusion.51
  412.3 1.5 fusion.53
  414.7 254.1 %all-reduce.6.cloned.1.call-done = f32[8,128,32]{1,2,0:T(8,128)} async-done(((f32[8,128,32]{1,2,0:T(8,128)}), f32[8,128,32]{1,2,0:T(8,128)}) %all-reduce.6.cloned.1.call-update) | async-done | bytes 131088 | tf_op jit(solution)/shard_map/psum | solution.py:70
  668.7 1.7 fusion.21
  670.4 454.8 %all-reduce.8.cloned.1.call-done = f32[16,1,1,128,32]{3,4,2,1,0:T(8,128)} async-done(((f32[16,1,1,128,32]{3,4,2,1,0:T(8,128)}), f32[16,1,1,128,32]{3,4,2,1,0:T(8,128)}) %all-reduce.8.cloned.1.call-update) | async-done | bytes 262160 | tf_op jit(solution)/shard_map/psum | solution.py:75
  1125.2 28.7 %all_to_all.8 = f32[16,1,1,128,32]{3,4,2,1,0:T(8,128)S(1)} all-to-all(f32[16,1,1,128,32]{3,4,2,1,0:T(8,128)} %all-reduce.8.cloned.1.call-done), channel_id=1, replica_groups=mesh['row'=16,'col'=32] {'row'}, dimensions={0} | all-to-all | bytes 524288 | tf_op jit(solution)/shard_map/all_to_all | solution.py:77
  (112 shorter events, 58.2 us)
Async XLA Ops:
  8.3 33.4 %all-to-all-start = ((f32[1,16,128,32]{2,3,0,1:T(8,128)}), f32[1,16,128,32]{2,3,0,1:T(8,128)S(1)}, u32[]{:S(2)}, u32[]{:S(2)}) async-start(f32[1,16,128,32]{2,3,0,1:T(8,128)} %copy.11), calls=%async_computation | async-start | bytes 524288 | tf_op jit(solution)/shard_map/all_to_all | solution.py:26
  26.4 268.7 %all-reduce.4.cloned.1.call-start = ((), (), s32[]{:S(2)}) async-start(), calls=%async_computation.2 | async-start | bytes 262144 | tf_op jit(solution)/shard_map/psum | solution.py:9
  42.4 626.3 %all-reduce.6.cloned.1.call-start = ((), (), s32[]{:S(2)}) async-start(), calls=%async_computation.3 | async-start | bytes 262144 | tf_op jit(solution)/shard_map/psum | solution.py:70
  413.8 0.7 copy-start
  414.5 710.7 %all-reduce.8.cloned.1.call-start = ((), (), s32[]{:S(2)}) async-start(), calls=%async_computation.4 | async-start | bytes 524288 | tf_op jit(solution)/shard_map/psum | solution.py:75
Sparse Core Ops, SparseCore 0:
  42.5 252.4 all-reduce.3
  414.6 254.0 all-reduce.5
  671.6 453.5 all-reduce.7
where the time goes:
time: 1170 us; the launch traced here: 1160 us
  waiting for transfers between devices  975 us (83%)
  matrix products  76.5 us (7%)
  blocking collectives  28.7 us (2%)
  other arithmetic  26.2 us (2%)
  local copies, waits for them, and re-layouts  23 us (2%)
  starting transfers between devices  18.2 us (2%)
  between operations  13.2 us (1%)
    psum x1, waiting for transfers between devices, per_device(): summed = lax.psum(total, 'col')  455 us
    psum x1, waiting for transfers between devices, per_device(): col_total = lax.psum(col_part, 'row')  254 us
    psum x1, waiting for transfers between devices, broadcast(): return lax.psum(kept, axis)  252 us
    dot_general x16, matrix products, step(): jnp.einsum('if,cjf->cij', frow, col_feats, precision=hi)  31.3 us
    all_to_all x1, blocking collectives, per_device(): lax.all_to_all(sectioned, 'row', split_axis=0, concat_axis=2, tiled=True)  28.7 us
    dot_general x16, matrix products, step(): jnp.einsum('cij,cjf->if', weight, col_feats, precision=hi)  24.1 us
  transfers between devices with their start and end apart: 4, of which 4 were waited for; matrix products, arithmetic and copies ran while one was open for 0% of the time, Pallas kernels for 0%

commit v1 on v0

v1 whole, which is shorter than its diff:
```python
import functools
import math

import jax
import jax.numpy as jnp
from jax import lax
from jax.experimental import pallas as pl
from jax.experimental.pallas import tpu as pltpu
from jax.sharding import PartitionSpec as P

F32, BF16, I32 = jnp.float32, jnp.bfloat16, jnp.int32
MESH = pl.DeviceIdType.MESH
C0 = 0.5 * math.log2(math.e)
C1 = 0.25 * math.log2(math.e)
NP = 4
NS = 16 // NP
BASE = (8 - NP) // 2
FAR = -1e30


def split3(x):
    h = x.astype(BF16).astype(F32)
    m = (x - h).astype(BF16).astype(F32)
    return h, m, (x - h - m).astype(BF16).astype(F32)


def pick(rows, n):
    sub = lax.broadcasted_iota(I32, (8, n), 0)
    out = jnp.zeros((8, n), F32)
    for k, v in enumerate(rows):
        out = jnp.where(sub == k, v, out)
    return out


def row_operand(f, a):
    h, m, l = split3(C0 * f)
    s = split3(-C1 * jnp.sum(f * f, axis=0, keepdims=True))
    one = jnp.ones_like(s[0])
    hot = (lax.broadcasted_iota(I32, (16, 128), 0) == a).astype(F32)
    return jnp.concatenate([h, h, m, h, m, l, pick([*s, one, one, one], 128), hot, jnp.zeros((40, 128), F32)], axis=0)


def col_operand(f, pen):
    h, m, l = split3(f)
    s = split3(-C1 * jnp.sum(f * f, axis=0, keepdims=True))
    one = jnp.ones_like(s[0])
    return jnp.concatenate([h, m, h, l, m, h, pick([one, one, one, *s], 128), pen, jnp.zeros((40, 128), F32)], axis=0)


def sides(f):
    h, m, _ = split3(f)
    one = pick([jnp.ones((1, 128), F32)], 128)
    pad = jnp.zeros((56, 128), F32)
    return jnp.concatenate([h, m, one, pad], axis=0), jnp.concatenate([h, jnp.zeros((32, 128), F32), one, pad], axis=0)


def dot(a, b):
    return lax.dot_general(a, b, (((1,), (0,)), ((), ())), preferred_element_type=F32)


def dev(zh, x, k, y, zl):
    return (zh * 8 + x * 2 + k, y * 8 + zl)


def push(src, dst, ss, rs, to):
    pltpu.make_async_remote_copy(
        src_ref=src, dst_ref=dst, send_sem=ss, recv_sem=rs, device_id=to, device_id_type=MESH
    ).start()


def arrived(ref, sem):
    pltpu.make_async_copy(ref, ref, sem).wait()


def kernel(
    tos, ft, adj_hbm, out,
    adj, rowf, colf, copb, ctt, acc, rowp, yrecv, ysum, zrecv, colp, krecv, csum, xrecv, c2, crecv, fin,
    s_adj, s_loc, s_row, s_col, s_c4, s_c5, s_far, s_yag, s_yr, s_z, s_k, s_x, s_c, s_ag, s_out, q_in, q_yr, q_z, q_k, q_x, q_c, q_ag,
):
    r = lax.axis_index("row")
    c = lax.axis_index("col")
    zh, x, k = r // 8, lax.rem(r // 2, 4), lax.rem(r, 2)
    y, zl = c // 8, lax.rem(c, 8)
    c16 = lax.rem(c, 16)
    wk = y // 2
    oz = 1 - zh
    pi, rho = lax.rem(r, NP), r // NP
    place = zl - BASE
    final = (place >= 0) & (place < NP)
    edge = (zl == 0) | (zl == 7)
    plane = [(lax.rem(x + d // 2, 4), lax.rem(k + d, 2)) for d in range(1, 8)]
    cpi, crho = lax.rem(c16, NP), c16 // NP

    for j in range(8):
        pltpu.make_async_copy(adj_hbm.at[pl.ds(2 * j, 2)], adj.at[pl.ds(2 * j, 2)], s_adj.at[j]).start()
    pltpu.make_async_copy(ft.at[:, r], rowf.at[:, r], s_loc.at[0]).start()

    @pl.when(k == wk)
    def _():
        pltpu.make_async_copy(ft.at[:, c16], colf.at[:, zh * 4 + x], s_loc.at[1]).start()

    bar = pltpu.get_barrier_semaphore()

    def tell(to):
        pl.semaphore_signal(bar, inc=1, device_id=to, device_id_type=MESH)

    for px, pk in plane:
        tell(dev(zh, px, pk, y, zl))
    for d in range(1, 4):
        tell(dev(zh, x, k, lax.rem(y + d, 4), zl))
    near = jnp.where(zl >= 4, 0, 7)
    for j in range(8):
        tell(dev(oz, j // 2, j % 2, y, near))
    for j in range(NP):
        @pl.when(zl != BASE + j)
        def _():
            tell(dev(zh, x, k, y, BASE + j))

    @pl.when(final)
    def _():
        def rows(j, _):
            q, z = j // 8, lax.rem(j, 8)
            sr = q * NP + place

            @pl.when((sr != r) | (z != zl))
            def _():
                tell((sr, y * 8 + z))
            return 0

        lax.fori_loop(0, NS * 8, rows, 0)

        def cols(j, _):
            q, h = j // 2, lax.rem(j, 2)
            sr = q * NP + place
            sy, sz, sk = 2 * k + sr // 8, lax.rem(sr, 8), y // 2
            to = dev(h, x, sk, sy, sz)

            @pl.when((to[0] != r) | (to[1] != c))
            def _():
                tell(to)
            return 0

        lax.fori_loop(0, NS * 2, cols, 0)

    wait_for = 10 + jnp.where(edge, 32, 0) + 16 + jnp.where(final, 7, 0)
    wait_for -= jnp.where(zl == BASE + pi, 1, 0)
    col_place = BASE + cpi
    col_self = (k == wk) & (zl == col_place) & (y // 2 == k)
    for g in range(2):
        wait_for += jnp.where((k == wk) & (zl == col_place) & (y == 2 * k + g), 1, 2)
    del col_self
    pl.semaphore_wait(bar, wait_for)

    @pl.when(edge)
    def _():
        first = jnp.where(zl == 0, 4, 0)

        @pl.when(k == wk)
        def _():
            for j in range(4):
                push(ft.at[:, lax.rem(y, 2) * 8 + first + j], colf.at[:, zh * 4 + x], q_in.at[0], s_c4, dev(oz, x, k, y, first + j))

        def far(j, _):
            t = oz * 8 + lax.rem(j, 8)
            push(ft.at[y, t], rowf.at[y, r], q_in.at[1], s_far, (t, y * 8 + first + j // 8))
            return 0

        lax.fori_loop(0, 32, far, 0)

    @pl.when(k == wk)
    def _():
        for px, pk in plane:
            push(ft.at[:, c16], colf.at[:, zh * 4 + x], q_in.at[2], s_col, dev(zh, px, pk, y, zl))

    for px, pk in plane:
        push(ft.at[:, zh * 8 + px * 2 + pk], rowf.at[:, r], q_in.at[3], s_row, dev(zh, px, pk, y, zl))

    sub = lax.broadcasted_iota(I32, (16, 128), 0)
    tile = jnp.zeros((16, 128), I32)
    for a in range(16):
        tile = jnp.where(sub == a, tos[a * 16 + r], tile)

    for j in range(8):
        arrived(adj.at[pl.ds(2 * j, 2)], s_adj.at[j])

    @pl.when(r == c16)
    def _():
        low = lax.broadcasted_iota(I32, (128, 128), 0) >= lax.broadcasted_iota(I32, (128, 128), 1)
        for b in range(8):
            a = 2 * b + c // 16
            adj[a, b] = jnp.where(low, adj[a, b].astype(F32), 0.0).astype(BF16)

    acc[...] = jnp.zeros_like(acc)
    arrived(rowf.at[:, r], s_loc.at[0])

    @pl.when(k == wk)
    def _():
        arrived(colf.at[:, zh * 4 + x], s_loc.at[1])
        arrived(colf.at[:, oz * 4 + x], s_c4)
        for px, pk in plane:
            push(colf.at[:, oz * 4 + x], colf.at[:, oz * 4 + x], q_in.at[4], s_c5, dev(zh, px, pk, y, zl))

    arrived(rowf.at[y, pl.ds(oz * 8, 8)], s_far)
    for d in range(1, 4):
        push(rowf.at[y, pl.ds(oz * 8, 8)], rowf.at[y, pl.ds(oz * 8, 8)], q_in.at[5], s_yag.at[d - 1], dev(zh, x, k, lax.rem(y + d, 4), zl))

    @pl.when(k == wk)
    def _():
        arrived(colf.at[:, pl.ds(0, 3)], s_col)
        arrived(colf.at[:, pl.ds(0, 3)], s_c5)

    @pl.when(k != wk)
    def _():
        arrived(colf.at[:, pl.ds(0, 4)], s_col)
        arrived(colf.at[:, pl.ds(0, 4)], s_c5)

    for b in range(8):
        f = colf[:, b].reshape(32, 128)
        ok = (tile > tos[b * 32 + c]) | (sub * 16 + r == b * 32 + c)
        copb[:, b * 128 : (b + 1) * 128] = col_operand(f, jnp.where(ok, 0.0, FAR)).astype(BF16)
        s1, s2 = sides(f)
        ctt[b * 128 : (b + 1) * 128, :] = s1.T.astype(BF16)
        ctt[1024 + b * 128 : 1024 + (b + 1) * 128, :] = s2.T.astype(BF16)

    def pair(j, _):
        a0 = 2 * j
        fs = [rowf[:, a0 + t].reshape(32, 128) for t in range(2)]
        lhs = jnp.concatenate([row_operand(fs[t], a0 + t).T.astype(BF16) for t in range(2)], axis=0)
        sd = [sides(f) for f in fs]
        g = jnp.concatenate([sd[t][u][:80] for u in range(2) for t in range(2)], axis=1).astype(BF16)
        e = jnp.exp2(dot(lhs, copb[...]))
        ad = jnp.concatenate([jnp.concatenate([adj[a0 + t, b] for b in range(8)], axis=1) for t in range(2)], axis=0)
        w = ad.astype(F32) * e
        wh = w.astype(BF16)
        wl = (w - wh.astype(F32)).astype(BF16)
        acc[...] += dot(g, jnp.concatenate([wh, wl], axis=0))
        p = dot(jnp.concatenate([wh, wl], axis=1), ctt[...])
        for t in range(2):
            q = p[t * 128 : (t + 1) * 128].T
            rowp[:, a0 + t] = (q[64:65] * fs[t] - q[0:32] - q[32:64]).reshape(4, 8, 128)
        for d in range(1, 4):
            py = lax.rem(y + d, 4)
            push(rowp.at[py, pl.ds(a0, 2)], yrecv.at[d - 1, pl.ds(a0, 2)], q_yr.at[j], s_yr.at[j], dev(zh, x, k, py, zl))
        return 0

    def settle(j, _):
        a0 = 2 * j
        arrived(yrecv.at[:, pl.ds(a0, 2)], s_yr.at[j])
        two = pl.ds(a0, 2)
        ysum[two] = (rowp[y, two] + yrecv[0, two]) + (yrecv[1, two] + yrecv[2, two])
        for t in range(2):
            a = a0 + t
            here = (a == r) & (zl == BASE + pi)

            @pl.when(here)
            def _():
                cp = pltpu.make_async_copy(ysum.at[a], zrecv.at[rho, zl], s_loc.at[2])
                cp.start()
                cp.wait()

            @pl.when(jnp.logical_not(here))
            def _():
                push(ysum.at[a], zrecv.at[rho, zl], q_z, s_z, (a, y * 8 + BASE + pi))
        return 0

    arrived(rowf.at[:, pl.ds(zh * 8, 7)], s_row)
    lax.fori_loop(zh * 4, zh * 4 + 4, pair, 0)
    for d in range(1, 4):
        arrived(rowf.at[lax.rem(y + 4 - d, 4), pl.ds(oz * 8, 8)], s_yag.at[d - 1])
    lax.fori_loop(zh * 4, zh * 4 + 4, settle, 0)
    lax.fori_loop(oz * 4, oz * 4 + 4, pair, 0)

    for b in range(8):
        q = acc[:, b * 128 : (b + 1) * 128]
        f = colf[:, b].reshape(32, 128)
        colp[:, b] = (q[64:65] * f - q[0:32] - q[32:64]).reshape(4, 8, 128)
    push(colp.at[pl.ds(2 * (1 - k), 2)], krecv, q_k, s_k, dev(zh, x, 1 - k, y, zl))
    arrived(krecv, s_k)
    csum[...] = (colp[pl.ds(2 * k, 2)] + krecv[...]).reshape(2, 2, 4, 8, 128)
    for d in range(1, 4):
        px = lax.rem(x + d, 4)
        push(csum.at[:, :, px], xrecv.at[d - 1], q_x, s_x, dev(zh, px, k, y, zl))
    lax.fori_loop(oz * 4, oz * 4 + 4, settle, 0)
    arrived(xrecv, s_x)
    c2[...] = (csum[:, :, x] + xrecv[0]) + (xrecv[1] + xrecv[2])
    for g in range(2):
        for h in range(2):
            to = dev(h, x, wk, 2 * k + g, col_place)
            here = (to[0] == r) & (to[1] == c)

            @pl.when(here)
            def _():
                cp = pltpu.make_async_copy(c2.at[g, h], crecv.at[crho, zh], s_loc.at[3])
                cp.start()
                cp.wait()

            @pl.when(jnp.logical_not(here))
            def _():
                push(c2.at[g, h], crecv.at[crho, zh], q_c, s_c, to)

    @pl.when(final)
    def _():
        mine = jnp.where(pi == place, 1, 0)

        @pl.when(mine == 1)
        def _():
            arrived(ysum.at[pl.ds(0, 1)], s_z) if NS * 8 == 2 else arrived(zrecv.reshape(NS * 8, 8, 128).at[pl.ds(0, NS * 8 - 1)], s_z)

        @pl.when(mine == 0)
        def _():
            arrived(zrecv, s_z)

        own = (k == wk) & (zl == col_place) & ((y == 2 * k) | (y == 2 * k + 1))

        @pl.when(own)
        def _():
            arrived(crecv.reshape(NS * 2, 8, 128).at[pl.ds(0, NS * 2 - 1)], s_c)

        @pl.when(jnp.logical_not(own))
        def _():
            arrived(crecv, s_c)

        for q in range(NS):
            t = crecv[q, 0] + crecv[q, 1]
            for z in range(8):
                t = t + zrecv[q, z]
            fin[q] = -0.5 * t
        pltpu.make_async_copy(fin, out.at[y, place], s_loc.at[4]).start()
        for d in range(1, 8):
            push(fin, out.at[y, place], q_ag.at[0], s_ag.at[place], dev(zh, x, k, y, lax.rem(zl + d, 8)))
        for d in range(1, 4):
            push(fin, out.at[y, place], q_ag.at[1], s_out.at[d - 1], dev(zh, x, k, lax.rem(y + d, 4), zl))
        arrived(out.at[y, place], s_loc.at[4])

    for j in range(NP):
        @pl.when(zl != BASE + j)
        def _():
            arrived(out.at[y, j], s_ag.at[j])
            for d in range(1, 4):
                push(out.at[y, j], out.at[y, j], q_ag.at[1], s_out.at[d - 1], dev(zh, x, k, lax.rem(y + d, 4), zl))
    for d in range(1, 4):
        arrived(out.at[lax.rem(y + 4 - d, 4)], s_out.at[d - 1])

    @pl.when(edge)
    def _():
        @pl.when(k == wk)
        def _():
            arrived(colf.at[:, pl.ds(0, 4)], q_in.at[0])
        arrived(rowf.at[:, pl.ds(0, 8)], q_in.at[1])

    @pl.when(k == wk)
    def _():
        arrived(colf.at[:, pl.ds(0, 7)], q_in.at[2])
        arrived(colf.at[:, pl.ds(0, 7)], q_in.at[4])
    arrived(colf.at[:, pl.ds(0, 7)], q_in.at[3])
    arrived(rowf.at[pl.ds(0, 3), pl.ds(0, 8)], q_in.at[5])
    for j in range(8):
        arrived(yrecv.at[:, pl.ds(0, 2)], q_yr.at[j])

    @pl.when(zl == BASE + pi)
    def _():
        arrived(ysum.at[pl.ds(0, 15)], q_z)

    @pl.when(zl != BASE + pi)
    def _():
        arrived(ysum, q_z)
    arrived(krecv, q_k)
    arrived(xrecv, q_x)
    own = (k == wk) & (zl == col_place) & ((y == 2 * k) | (y == 2 * k + 1))

    @pl.when(own)
    def _():
        arrived(c2.reshape(4, 8, 128).at[pl.ds(0, 3)], q_c)

    @pl.when(jnp.logical_not(own))
    def _():
        arrived(c2, q_c)

    @pl.when(final)
    def _():
        arrived(ysum.at[pl.ds(0, NS)].reshape(1, NS, 8, 128) if NS * 7 > 16 * 4 else yrecv.reshape(48, 8, 128).at[pl.ds(0, NS * 7)], q_ag.at[0])
    arrived(out.at[pl.ds(0, 3)], q_ag.at[1])


def per_device(adjoint, features, tile_of_slot):
    ft = features.T.reshape(4, 8, 16, 128).transpose(0, 2, 1, 3)
    adj = adjoint.reshape(16, 8, 128, 128)
    anyspace = pl.BlockSpec(memory_space=pl.ANY)
    dma, vm = pltpu.SemaphoreType.DMA, pltpu.VMEM
    out = pl.pallas_call(
        kernel,
        out_shape=jax.ShapeDtypeStruct((4, NP, NS, 8, 128), F32),
        in_specs=[pl.BlockSpec(memory_space=pltpu.SMEM), anyspace, anyspace],
        out_specs=anyspace,
        scratch_shapes=[
            vm((16, 8, 128, 128), BF16),
            vm((4, 16, 8, 128), F32),
            vm((4, 8, 8, 128), F32),
            vm((256, 1024), BF16),
            vm((2048, 128), BF16),
            vm((80, 1024), F32),
            vm((4, 16, 8, 128), F32),
            vm((3, 16, 8, 128), F32),
            vm((16, 8, 128), F32),
            vm((NS, 8, 8, 128), F32),
            vm((4, 8, 8, 128), F32),
            vm((2, 8, 8, 128), F32),
            vm((2, 2, 4, 8, 128), F32),
            vm((3, 2, 2, 8, 128), F32),
            vm((2, 2, 8, 128), F32),
            vm((NS, 2, 8, 128), F32),
            vm((NS, 8, 128), F32),
            dma((8,)), dma((5,)), dma, dma, dma, dma, dma, dma((3,)), dma((8,)), dma, dma, dma, dma, dma((NP,)), dma((3,)),
            dma((6,)), dma((8,)), dma, dma, dma, dma, dma((2,)),
        ],
        compiler_params=pltpu.CompilerParams(collective_id=0, has_side_effects=True, vmem_limit_bytes=60 << 20),
        cost_estimate=pl.CostEstimate(flops=5 * 2**30, bytes_accessed=5 << 20, transcendentals=2 << 20),
        name="gradient",
    )(tile_of_slot, ft, adj)
    return out.transpose(0, 3, 2, 1, 4).reshape(32, 2048).T


def solution(mesh):
    return jax.shard_map(
        per_device,
        mesh=mesh,
        in_specs=(P("row", None, "col", None, None, None), P("row", None), P()),
        out_specs=P("row", None),
        check_vma=False,
    )
```

time: 1170 us -> 59.8 us (0.05)
  waiting for transfers between devices: 975 us -> 0 us
  matrix products: 76.5 us -> 0 us
  Pallas kernels: 0 us -> 57.9 us
  blocking collectives: 28.7 us -> 0 us
  other arithmetic: 26.2 us -> 0 us
  local copies, waits for them, and re-layouts: 23 us -> 1.68 us
  starting transfers between devices: 18.2 us -> 0 us
  between operations: 13.2 us -> 0.01 us
    psum x3 -> x0, waiting for transfers between devices: 961 us -> none  [the longest x1 455 us: per_device(): summed = lax.psum(total, 'col')]
    dot_general x48 -> x0, matrix products: 76.5 us -> none  [the longest x16 31.3 us: step(): jnp.einsum('if,cjf->cij', frow, col_feats, precision=hi)]
    pallas_call x0 -> x1, Pallas kernels: none -> 57.9 us  [per_device(): pl.pallas_call(kernel, out_shape=jax.ShapeDtypeStruct((4, NP, NS, 8, 128)...]
    all_to_all x1 -> x0, blocking collectives: 28.7 us -> none  [per_device(): lax.all_to_all(sectioned, 'row', split_axis=0, concat_axis=2, tiled=True)]
    eq x16 -> x0, other arithmetic: 20.4 us -> none  [step(): diag = (col_slots == rslot)[:, None, None] & lower[None]]
    dynamic_slice x32 -> x0, local copies, waits for them, and re-layouts: 19.5 us -> none  [per_device(): lax.scan(step, jnp.zeros((nct, bsize, width), jnp.float32), (tiles_local,...]
    all_to_all x1 -> x0, starting transfers between devices: 18 us -> none  [per_device(): lax.all_to_all(local, 'row', split_axis=1, concat_axis=0, tiled=True)]
    all_to_all x1 -> x0, waiting for transfers between devices: 14.4 us -> none  [per_device(): lax.all_to_all(local, 'row', split_axis=1, concat_axis=0, tiled=True)]
  transfers between devices with their start and end apart: 4 -> 0, of which waited for: 4 -> 0; matrix products, arithmetic and copies ran while one was open for 0% -> 0% of each run, Pallas kernels for 0% -> 0%
where the time goes in v1:
time: 59.8 us; the launch traced here: 59.6 us
  Pallas kernels  57.9 us (97%)
  local copies, waits for them, and re-layouts  1.68 us (3%)
    pallas_call x1, Pallas kernels, per_device(): pl.pallas_call(kernel, out_shape=jax.ShapeDtypeStruct((4, NP, NS, 8, 128)...  57.9 us
    transpose x1, local copies, waits for them, and re-layouts, per_device(): return out.transpose(0, 3, 2, 1, 4).reshape(32, 2048).T  1.68 us

profile of v1, /device:TPU:6, one launch (start us, length us, event | category | flops | bytes accessed | tf_op | source)
XLA Modules:
  0.0 59.6 jit_solution(1274548038114845480)
XLA Ops:
  0.0 57.9 %gradient.1 = f32[4,4,4,8,128]{4,3,2,1,0:T(8,128)} custom-call(s32[256]{0:T(256)} %tos.1, f32[4,16,8,128]{3,2,1,0:T(8,128)} %bitcast.12, bf16[16,8,128,128]{3,2,1,0:T(8,128)(2,1)} %bitcast.11), custom_call_target="tpu_custom_call" | custom-call | flops 5368709120 | bytes 5242880 | tf_op jit(solution)/shard_map/gradient/pallas_call | solution.py:390
  57.9 1.7 %copy.4 = f32[4,8,4,4,128]{4,1,3,2,0:T(8,128)} copy(f32[4,8,4,4,128]{4,1,2,3,0:T(8,128)} %bitcast.10) | data formatting | bytes 524288 | tf_op jit(solution)/shard_map/transpose | solution.py:420

commit v2 on v1

v2 whole, which is shorter than its diff:
```python
import functools
import math

import jax
import jax.numpy as jnp
from jax import lax
from jax.experimental import pallas as pl
from jax.experimental.pallas import tpu as pltpu
from jax.sharding import PartitionSpec as P

F32, BF16, I32 = jnp.float32, jnp.bfloat16, jnp.int32
MESH = pl.DeviceIdType.MESH
C0 = 0.5 * math.log2(math.e)
C1 = 0.25 * math.log2(math.e)
NP = 4
NS = 16 // NP
BASE = (8 - NP) // 2
FAR = -1e30


def split3(x):
    h = x.astype(BF16).astype(F32)
    m = (x - h).astype(BF16).astype(F32)
    return h, m, (x - h - m).astype(BF16).astype(F32)


def pick(rows, n):
    sub = lax.broadcasted_iota(I32, (8, n), 0)
    out = jnp.zeros((8, n), F32)
    for k, v in enumerate(rows):
        out = jnp.where(sub == k, v, out)
    return out


def row_operand(f, a):
    h, m, l = split3(C0 * f)
    s = split3(-C1 * jnp.sum(f * f, axis=0, keepdims=True))
    one = jnp.ones_like(s[0])
    hot = (lax.broadcasted_iota(I32, (16, 128), 0) == a).astype(F32)
    return jnp.concatenate([h, h, m, h, m, l, pick([*s, one, one, one], 128), hot, jnp.zeros((40, 128), F32)], axis=0)


def col_operand(f, pen):
    h, m, l = split3(f)
    s = split3(-C1 * jnp.sum(f * f, axis=0, keepdims=True))
    one = jnp.ones_like(s[0])
    return jnp.concatenate([h, m, h, l, m, h, pick([one, one, one, *s], 128), pen, jnp.zeros((40, 128), F32)], axis=0)


def sides(f):
    h, m, _ = split3(f)
    one = pick([jnp.ones((1, 128), F32)], 128)
    pad = jnp.zeros((56, 128), F32)
    return jnp.concatenate([h, m, one, pad], axis=0), jnp.concatenate([h, jnp.zeros((32, 128), F32), one, pad], axis=0)


def dot(a, b):
    return lax.dot_general(a, b, (((1,), (0,)), ((), ())), preferred_element_type=F32)


def dev(zh, x, k, y, zl):
    return (zh * 8 + x * 2 + k, y * 8 + zl)


def push(src, dst, ss, rs, to):
    pltpu.make_async_remote_copy(
        src_ref=src, dst_ref=dst, send_sem=ss, recv_sem=rs, device_id=to, device_id_type=MESH
    ).start()


def arrived(ref, sem):
    pltpu.make_async_copy(ref, ref, sem).wait()


def kernel(
    tos, ft, adj_hbm, out,
    adj, rowf, colf, cop, ctt, lhs, gb, acc, prow, rowp, yrecv, ysum, zrecv, colp, krecv, csum, xrecv, c2, crecv, fin,
    s_adj, s_loc, s_row, s_col, s_c4, s_c5, s_far, s_yag, s_yr, s_z, s_k, s_x, s_c, s_ag, s_out,
    q_in, q_yr, q_z, q_k, q_x, q_c, q_ag, ready,
):
    r = lax.axis_index("row")
    c = lax.axis_index("col")
    zh, x, k = r // 8, lax.rem(r // 2, 4), lax.rem(r, 2)
    y, zl = c // 8, lax.rem(c, 8)
    c16 = lax.rem(c, 16)
    wk = y // 2
    oz = 1 - zh
    pi, rho = lax.rem(r, NP), r // NP
    cpi, crho = lax.rem(c16, NP), c16 // NP
    place = zl - BASE
    final = (place >= 0) & (place < NP)
    edge = (zl == 0) | (zl == 7)
    plane = [dev(zh, lax.rem(x + d // 2, 4), lax.rem(k + d, 2), y, zl) for d in range(1, 8)]
    plane_tile = [zh * 8 + lax.rem(x + d // 2, 4) * 2 + lax.rem(k + d, 2) for d in range(1, 8)]
    ys = [dev(zh, x, k, lax.rem(y + d, 4), zl) for d in range(1, 4)]
    line = []
    for d in (4, 3, 2, 1):
        for z in (lax.rem(zh * 8 + zl + d, 16), lax.rem(zh * 8 + zl + 16 - d, 16)):
            line.append(dev(z // 8, x, k, y, lax.rem(z, 8)))

    bar = pltpu.get_barrier_semaphore()

    def tell(sem, to):
        pl.semaphore_signal(sem, inc=1, device_id=to, device_id_type=MESH)

    near = jnp.where(zl >= 4, 0, 7)
    for j in range(8):
        tell(bar, dev(oz, j // 2, j % 2, y, near))
    for to in line + ys + plane:
        tell(bar, to)
    for j in range(8):
        pltpu.make_async_copy(adj_hbm.at[pl.ds(2 * j, 2)], adj.at[pl.ds(2 * j, 2)], s_adj.at[j]).start()
    pltpu.make_async_copy(ft.at[:, r], rowf.at[:, r], s_loc.at[0]).start()

    @pl.when(k == wk)
    def _():
        pltpu.make_async_copy(ft.at[:, c16], colf.at[:, zh * 4 + x], s_loc.at[1]).start()

    pl.semaphore_wait(bar, 18 + jnp.where(edge, 32, 0))

    @pl.when(edge)
    def _():
        low = jnp.where(zl == 0, 4, 3)
        up = jnp.where(zl == 0, 1, -1)

        @pl.when(k == wk)
        def _():
            for j in range(4):
                z = low + up * j
                push(ft.at[:, lax.rem(y, 2) * 8 + z], colf.at[:, zh * 4 + x], q_in.at[0], s_c4, dev(oz, x, k, y, z))

        def far(j, _):
            t = oz * 8 + lax.rem(j, 8)
            push(ft.at[y, t], rowf.at[y, r], q_in.at[1], s_far, (t, y * 8 + low + up * (j // 8)))
            return 0

        lax.fori_loop(0, 32, far, 0)

    @pl.when(k == wk)
    def _():
        for to in plane:
            push(ft.at[:, c16], colf.at[:, zh * 4 + x], q_in.at[2], s_col, to)

    for to, t in zip(plane, plane_tile, strict=True):
        push(ft.at[:, t], rowf.at[:, r], q_in.at[3], s_row, to)

    for to in line:
        tell(ready.at[0], to)

    sub = lax.broadcasted_iota(I32, (16, 128), 0)
    tile = jnp.zeros((16, 128), I32)
    for a in range(16):
        tile = jnp.where(sub == a, tos[a * 16 + r], tile)

    for j in range(8):
        arrived(adj.at[pl.ds(2 * j, 2)], s_adj.at[j])

    @pl.when(r == c16)
    def _():
        tri = lax.broadcasted_iota(I32, (128, 128), 0) >= lax.broadcasted_iota(I32, (128, 128), 1)
        for b in range(8):
            a = 2 * b + c // 16
            adj[a, b] = jnp.where(tri, adj[a, b].astype(F32), 0.0).astype(BF16)

    acc[...] = jnp.zeros_like(acc)

    def col_side(h):
        for u in range(4):
            b = (zh if h == 0 else oz) * 4 + u
            w = slice(u * 128, (u + 1) * 128)
            f = colf[:, b].reshape(32, 128)
            ok = (tile > tos[b * 32 + c]) | (sub * 16 + r == b * 32 + c)
            cop[h, :, w] = col_operand(f, jnp.where(ok, 0.0, FAR)).astype(BF16)
            s1, s2 = sides(f)
            ctt[h, u * 128 : (u + 1) * 128, :] = s1.T.astype(BF16)
            ctt[h, 512 + u * 128 : 512 + (u + 1) * 128, :] = s2.T.astype(BF16)

    def row_side(i, half):
        for t in range(2):
            a = half * 8 + 2 * i + t
            f = rowf[:, a].reshape(32, 128)
            lhs[i, t * 128 : (t + 1) * 128, :] = row_operand(f, a).T.astype(BF16)
            s1, s2 = sides(f)
            gb[i, :, t * 128 : (t + 1) * 128] = s1[:80].astype(BF16)
            gb[i, :, 256 + t * 128 : 256 + (t + 1) * 128] = s2[:80].astype(BF16)

    def quarter(i, half, h):
        a0 = half * 8 + 2 * i
        b0 = (zh if h == 0 else oz) * 4
        e = jnp.exp2(dot(lhs[i], cop[h]))
        ad = jnp.concatenate([jnp.concatenate([adj[a0 + t, b0 + u] for u in range(4)], axis=1) for t in range(2)], axis=0)
        w = ad.astype(F32) * e
        wh = w.astype(BF16)
        wl = (w - wh.astype(F32)).astype(BF16)
        acc[h] += dot(gb[i], jnp.concatenate([wh, wl], axis=0))
        return dot(jnp.concatenate([wh, wl], axis=1), ctt[h])

    def finish_rows(i, half, p):
        a0 = half * 8 + 2 * i
        for t in range(2):
            q = p[t * 128 : (t + 1) * 128].T
            f = rowf[:, a0 + t].reshape(32, 128)
            rowp[:, a0 + t] = (q[64:65] * f - q[0:32] - q[32:64]).reshape(4, 8, 128)
        two = pl.ds(a0, 2)
        for d in range(1, 4):
            push(rowp.at[lax.rem(y + d, 4), two], yrecv.at[d - 1, two], q_yr.at[a0 // 2], s_yr.at[a0 // 2], ys[d - 1])

    def settle(i, half):
        a0 = half * 8 + 2 * i
        two = pl.ds(a0, 2)
        arrived(yrecv.at[:, two], s_yr.at[a0 // 2])
        ysum[two] = (rowp[y, two] + yrecv[0, two]) + (yrecv[1, two] + yrecv[2, two])
        for t in range(2):
            a = a0 + t
            here = (a == r) & (zl == BASE + pi)

            @pl.when(here)
            def _():
                cp = pltpu.make_async_copy(ysum.at[a], zrecv.at[rho, zl], s_loc.at[2])
                cp.start()
                cp.wait()

            @pl.when(jnp.logical_not(here))
            def _():
                push(ysum.at[a], zrecv.at[rho, zl], q_z, s_z, (a, y * 8 + BASE + pi))

    arrived(rowf.at[:, r], s_loc.at[0])
    arrived(rowf.at[:, pl.ds(zh * 8, 7)], s_row)

    @pl.when(k == wk)
    def _():
        arrived(colf.at[:, zh * 4 + x], s_loc.at[1])
        arrived(colf.at[:, pl.ds(0, 3)], s_col)

    @pl.when(k != wk)
    def _():
        arrived(colf.at[:, pl.ds(0, 4)], s_col)

    col_side(0)

    @pl.when(k == wk)
    def _():
        arrived(colf.at[:, oz * 4 + x], s_c4)
        for to in plane:
            push(colf.at[:, oz * 4 + x], colf.at[:, oz * 4 + x], q_in.at[4], s_c5, to)

    def own_own(i, _):
        row_side(i, zh)
        prow[i] = quarter(i, zh, 0)

        @pl.when(i == 1)
        def _():
            arrived(rowf.at[y, pl.ds(oz * 8, 8)], s_far)
            mine = rowf.at[y, pl.ds(oz * 8, 8)]
            for d in range(1, 4):
                push(mine, mine, q_in.at[5], s_yag.at[d - 1], ys[d - 1])
        return 0

    lax.fori_loop(0, 4, own_own, 0)

    pl.semaphore_wait(ready.at[0], 8)
    for to in plane + ys:
        tell(ready.at[1], to)

    @pl.when(k == wk)
    def _():
        arrived(colf.at[:, pl.ds(0, 3)], s_c5)

    @pl.when(k != wk)
    def _():
        arrived(colf.at[:, pl.ds(0, 4)], s_c5)

    col_side(1)

    def own_other(i, _):
        finish_rows(i, zh, prow[i] + quarter(i, zh, 1))
        return 0

    lax.fori_loop(0, 4, own_other, 0)

    for d in range(1, 4):
        arrived(rowf.at[lax.rem(y + 4 - d, 4), pl.ds(oz * 8, 8)], s_yag.at[d - 1])

    def other_other(i, _):
        row_side(i, oz)
        prow[i] = quarter(i, oz, 1)
        return 0

    lax.fori_loop(0, 4, other_other, 0)

    def col_terms(h):
        half = zh if h == 0 else oz
        for u in range(4):
            q = acc[h, :, u * 128 : (u + 1) * 128]
            f = colf[:, half * 4 + u].reshape(32, 128)
            colp[h, :, u] = (q[64:65] * f - q[0:32] - q[32:64]).reshape(4, 8, 128)

        @pl.when(k != wk)
        def _():
            push(colp.at[h], krecv.at[h], q_k.at[h], s_k.at[h], dev(zh, x, wk, y, zl))

    def col_x(h):
        @pl.when(k == wk)
        def _():
            arrived(krecv.at[h], s_k.at[h])
            csum[h] = colp[h] + krecv[h]
            for d in range(1, 4):
                px = lax.rem(x + d, 4)
                push(csum.at[h, :, px], xrecv.at[h, d - 1], q_x.at[h], s_x.at[h], dev(zh, px, k, y, zl))

    def col_out(h):
        half = zh if h == 0 else oz

        @pl.when(k == wk)
        def _():
            arrived(xrecv.at[h], s_x.at[h])
            c2[h] = (csum[h, :, x] + xrecv[h, 0]) + (xrecv[h, 1] + xrecv[h, 2])
            for g in range(4):
                here = (y == g) & (zl == BASE + cpi) if h == 0 else None
                to = dev(half, x, k, g, BASE + cpi)
                if h == 0:
                    @pl.when(here)
                    def _():
                        cp = pltpu.make_async_copy(c2.at[h, g], crecv.at[crho, zh], s_loc.at[3])
                        cp.start()
                        cp.wait()

                    @pl.when(jnp.logical_not(here))
                    def _():
                        push(c2.at[h, g], crecv.at[crho, zh], q_c, s_c, to)
                else:
                    push(c2.at[h, g], crecv.at[crho, zh], q_c, s_c, to)

    col_terms(1)
    pl.semaphore_wait(ready.at[1], 10)

    def other_own(i, _):
        finish_rows(i, oz, prow[i] + quarter(i, oz, 0))

        @pl.when(i == 1)
        def _():
            col_x(1)
        settle(i, zh)
        return 0

    lax.fori_loop(0, 4, other_own, 0)

    col_terms(0)
    col_x(0)

    settle(0, oz)
    settle(1, oz)

    col_out(1)

    settle(2, oz)
    settle(3, oz)

    col_out(0)

    @pl.when(final)
    def _():
        @pl.when(pi == place)
        def _():
            arrived(zrecv.reshape(NS * 8, 8, 128).at[pl.ds(0, NS * 8 - 1)], s_z)

        @pl.when(pi != place)
        def _():
            arrived(zrecv, s_z)

        @pl.when((k == wk) & (cpi == place))
        def _():
            arrived(crecv.reshape(NS * 2, 8, 128).at[pl.ds(0, NS * 2 - 1)], s_c)

        @pl.when((k != wk) | (cpi != place))
        def _():
            arrived(crecv, s_c)

        for q in range(NS):
            t = crecv[q, 0] + crecv[q, 1]
            for z in range(8):
                t = t + zrecv[q, z]
            fin[q] = -0.5 * t
        pltpu.make_async_copy(fin, out.at[y, :, place], s_loc.at[4]).start()
        for d in range(1, 8):
            push(fin, out.at[y, :, place], q_ag.at[0], s_ag.at[place], dev(zh, x, k, y, lax.rem(zl + d, 8)))
        for d in range(1, 4):
            push(fin, out.at[y, :, place], q_ag.at[1], s_out.at[d - 1], ys[d - 1])
        arrived(out.at[y, :, place], s_loc.at[4])

    for j in range(NP):
        @pl.when(zl != BASE + j)
        def _():
            arrived(out.at[y, :, j], s_ag.at[j])
            for d in range(1, 4):
                push(out.at[y, :, j], out.at[y, :, j], q_ag.at[1], s_out.at[d - 1], ys[d - 1])

    for d in range(1, 4):
        arrived(out.at[lax.rem(y + 4 - d, 4)], s_out.at[d - 1])

    @pl.when(edge)
    def _():
        @pl.when(k == wk)
        def _():
            arrived(colf.at[:, pl.ds(0, 4)], q_in.at[0])
        arrived(rowf.at[:, pl.ds(0, 8)], q_in.at[1])

    @pl.when(k == wk)
    def _():
        arrived(colf.at[:, pl.ds(0, 7)], q_in.at[2])
        arrived(colf.at[:, pl.ds(0, 7)], q_in.at[4])
        for h in range(2):
            arrived(xrecv.at[h], q_x.at[h])

    @pl.when(k != wk)
    def _():
        for h in range(2):
            arrived(krecv.at[h], q_k.at[h])
    arrived(colf.at[:, pl.ds(0, 7)], q_in.at[3])
    arrived(rowf.at[pl.ds(0, 3), pl.ds(0, 8)], q_in.at[5])
    for j in range(8):
        arrived(yrecv.at[:, pl.ds(0, 2)], q_yr.at[j])

    @pl.when(zl == BASE + pi)
    def _():
        arrived(ysum.at[pl.ds(0, 15)], q_z)

    @pl.when(zl != BASE + pi)
    def _():
        arrived(ysum, q_z)

    @pl.when((k == wk) & (zl == BASE + cpi))
    def _():
        arrived(c2.reshape(8, 8, 128).at[pl.ds(0, 7)], q_c)

    @pl.when((k == wk) & (zl != BASE + cpi))
    def _():
        arrived(c2, q_c)

    @pl.when(final)
    def _():
        arrived(zrecv.reshape(NS * 8, 8, 128).at[pl.ds(0, NS * 7)], q_ag.at[0])
    arrived(out.at[pl.ds(0, 3)], q_ag.at[1])


def per_device(adjoint, features, tile_of_slot):
    ft = features.T.reshape(4, 8, 16, 128).transpose(0, 2, 1, 3)
    adj = adjoint.reshape(16, 8, 128, 128)
    anyspace = pl.BlockSpec(memory_space=pl.ANY)
    dma, vm = pltpu.SemaphoreType.DMA, pltpu.VMEM
    out = pl.pallas_call(
        kernel,
        out_shape=jax.ShapeDtypeStruct((4, NS, NP, 8, 128), F32),
        in_specs=[pl.BlockSpec(memory_space=pltpu.SMEM), anyspace, anyspace],
        out_specs=anyspace,
        scratch_shapes=[
            vm((16, 8, 128, 128), BF16),
            vm((4, 16, 8, 128), F32),
            vm((4, 8, 8, 128), F32),
            vm((2, 256, 512), BF16),
            vm((2, 1024, 128), BF16),
            vm((4, 256, 256), BF16),
            vm((4, 80, 512), BF16),
            vm((2, 80, 512), F32),
            vm((4, 256, 128), F32),
            vm((4, 16, 8, 128), F32),
            vm((3, 16, 8, 128), F32),
            vm((16, 8, 128), F32),
            vm((NS, 8, 8, 128), F32),
            vm((2, 4, 4, 8, 128), F32),
            vm((2, 4, 4, 8, 128), F32),
            vm((2, 4, 4, 8, 128), F32),
            vm((2, 3, 4, 8, 128), F32),
            vm((2, 4, 8, 128), F32),
            vm((NS, 2, 8, 128), F32),
            vm((NS, 8, 128), F32),
            dma((8,)), dma((5,)), dma, dma, dma, dma, dma, dma((3,)), dma((8,)), dma, dma((2,)), dma((2,)), dma, dma((NP,)), dma((3,)),
            dma((6,)), dma((8,)), dma, dma((2,)), dma((2,)), dma, dma((2,)), pltpu.SemaphoreType.REGULAR((2,)),
        ],
        compiler_params=pltpu.CompilerParams(collective_id=0, has_side_effects=True, vmem_limit_bytes=60 << 20),
        cost_estimate=pl.CostEstimate(flops=5 * 2**30, bytes_accessed=5 << 20, transcendentals=2 << 20),
        name="gradient",
    )(tile_of_slot, ft, adj)
    return out.reshape(4, 16, 8, 128).transpose(0, 2, 1, 3).reshape(32, 2048).T


def solution(mesh):
    return jax.shard_map(
        per_device,
        mesh=mesh,
        in_specs=(P("row", None, "col", None, None, None), P("row", None), P()),
        out_specs=P("row", None),
        check_vma=False,
    )
```

time: 59.8 us -> 55.9 us (0.935)
  Pallas kernels: 57.9 us -> 53.9 us
    pallas_call x1, Pallas kernels: 57.9 us -> 53.9 us  [per_device(): pl.pallas_call(kernel, out_shape=jax.ShapeDtypeStruct((4, NS, NP, 8, 128)...]
    transpose x1 -> x0, local copies, waits for them, and re-layouts: 1.68 us -> none  [per_device(): return out.transpose(0, 3, 2, 1, 4).reshape(32, 2048).T]
    unnamed x0 -> x1, local copies, waits for them, and re-layouts: none -> 1.67 us
where the time goes in v2:
time: 55.9 us; the launch traced here: 55.6 us
  Pallas kernels  53.9 us (96%)
  local copies, waits for them, and re-layouts  1.67 us (3%)
    pallas_call x1, Pallas kernels, per_device(): pl.pallas_call(kernel, out_shape=jax.ShapeDtypeStruct((4, NS, NP, 8, 128)...  53.9 us
    unnamed x1, local copies, waits for them, and re-layouts  1.67 us

profile of v2, /device:TPU:6, one launch (start us, length us, event | category | flops | bytes accessed | tf_op | source)
XLA Modules:
  0.0 55.6 jit_solution(11984134456348373393)
XLA Ops:
  0.0 53.9 %gradient.1 = f32[4,4,4,8,128]{4,3,2,1,0:T(8,128)} custom-call(s32[256]{0:T(256)} %tos.1, f32[4,16,8,128]{3,2,1,0:T(8,128)} %bitcast.15, bf16[16,8,128,128]{3,2,1,0:T(8,128)(2,1)} %bitcast.14), custom_call_target="tpu_custom_call" | custom-call | flops 5368709120 | bytes 5242880 | tf_op jit(solution)/shard_map/gradient/pallas_call | solution.py:451
  53.9 1.7 %copy.5 = f32[2048,32]{0,1:T(8,128)} copy(f32[2048,32]{0,1:T(8,128)} %bitcast.13) | data formatting | bytes 524288

commit v3 on v2

--- a/solution.py
+++ b/solution.py
@@ -73,9 +73,9 @@
 
 
 def kernel(
-    tos, ft, adj_hbm, out,
-    adj, rowf, colf, cop, ctt, lhs, gb, acc, prow, rowp, yrecv, ysum, zrecv, colp, krecv, csum, xrecv, c2, crecv, fin,
-    s_adj, s_loc, s_row, s_col, s_c4, s_c5, s_far, s_yag, s_yr, s_z, s_k, s_x, s_c, s_ag, s_out,
+    tos_hbm, ft, adj_hbm, out,
+    tos, adj, ftv, rowf, colf, far, zbuf, cop, ctt, lhs, gb, acc, prow, rowp, yrecv, ysum, zrecv, colp, krecv, csum, xrecv, c2, crecv, fin,
+    s_adj, s_loc, s_row, s_col, s_c4, s_c5, s_far, s_oth, s_yr, s_z, s_k, s_x, s_c, s_ag, s_out,
     q_in, q_yr, q_z, q_k, q_x, q_c, q_ag, ready,
 ):
     r = lax.axis_index("row")
@@ -93,6 +93,9 @@
     plane = [dev(zh, lax.rem(x + d // 2, 4), lax.rem(k + d, 2), y, zl) for d in range(1, 8)]
     plane_tile = [zh * 8 + lax.rem(x + d // 2, 4) * 2 + lax.rem(k + d, 2) for d in range(1, 8)]
     ys = [dev(zh, x, k, lax.rem(y + d, 4), zl) for d in range(1, 4)]
+    def order(i):
+        return lax.rem(x + jnp.where(i == 0, 2, jnp.where(i == 1, 1, jnp.where(i == 2, 3, 0))), 4)
+
     line = []
     for d in (4, 3, 2, 1):
         for z in (lax.rem(zh * 8 + zl + d, 16), lax.rem(zh * 8 + zl + 16 - d, 16)):
@@ -103,50 +106,48 @@
     def tell(sem, to):
         pl.semaphore_signal(sem, inc=1, device_id=to, device_id_type=MESH)
 
-    near = jnp.where(zl >= 4, 0, 7)
-    for j in range(8):
-        tell(bar, dev(oz, j // 2, j % 2, y, near))
     for to in line + ys + plane:
         tell(bar, to)
     for j in range(8):
         pltpu.make_async_copy(adj_hbm.at[pl.ds(2 * j, 2)], adj.at[pl.ds(2 * j, 2)], s_adj.at[j]).start()
-    pltpu.make_async_copy(ft.at[:, r], rowf.at[:, r], s_loc.at[0]).start()
-
-    @pl.when(k == wk)
-    def _():
-        pltpu.make_async_copy(ft.at[:, c16], colf.at[:, zh * 4 + x], s_loc.at[1]).start()
-
-    pl.semaphore_wait(bar, 18 + jnp.where(edge, 32, 0))
+    pltpu.make_async_copy(ft, ftv, s_loc.at[0]).start()
+    pltpu.make_async_copy(tos_hbm, tos, s_loc.at[1]).start()
+
+    pl.semaphore_wait(bar, 18)
+    arrived(ftv, s_loc.at[0])
 
     @pl.when(edge)
     def _():
         low = jnp.where(zl == 0, 4, 3)
         up = jnp.where(zl == 0, 1, -1)
 
-        @pl.when(k == wk)
-        def _():
-            for j in range(4):
-                z = low + up * j
-                push(ft.at[:, lax.rem(y, 2) * 8 + z], colf.at[:, zh * 4 + x], q_in.at[0], s_c4, dev(oz, x, k, y, z))
-
-        def far(j, _):
-            t = oz * 8 + lax.rem(j, 8)
-            push(ft.at[y, t], rowf.at[y, r], q_in.at[1], s_far, (t, y * 8 + low + up * (j // 8)))
-            return 0
-
-        lax.fori_loop(0, 32, far, 0)
+        for j in range(4):
+            z = low + up * j
+
+            @pl.when(k == wk)
+            def _():
+                push(ftv.at[:, lax.rem(y, 2) * 8 + z], colf.at[:, zh * 4 + x], q_in.at[0], s_c4, dev(oz, x, k, y, z))
+
+        for j in range(4):
+            push(ftv.at[y, pl.ds(oz * 8, 8)], far, q_in.at[1], s_far, dev(oz, x, k, y, low + up * j))
 
     @pl.when(k == wk)
     def _():
         for to in plane:
-            push(ft.at[:, c16], colf.at[:, zh * 4 + x], q_in.at[2], s_col, to)
+            push(ftv.at[:, c16], colf.at[:, zh * 4 + x], q_in.at[2], s_col, to)
 
     for to, t in zip(plane, plane_tile, strict=True):
-        push(ft.at[:, t], rowf.at[:, r], q_in.at[3], s_row, to)
-
-    for to in line:
+        push(ftv.at[:, t], rowf.at[:, r], q_in.at[3], s_row, to)
+
+    for to in line + ys:
         tell(ready.at[0], to)
-
+    rowf[:, r] = ftv[:, r]
+
+    @pl.when(k == wk)
+    def _():
+        colf[:, zh * 4 + x] = ftv[:, c16]
+
+    arrived(tos, s_loc.at[1])
     sub = lax.broadcasted_iota(I32, (16, 128), 0)
     tile = jnp.zeros((16, 128), I32)
     for a in range(16):
@@ -177,7 +178,7 @@
 
     def row_side(i, half):
         for t in range(2):
-            a = half * 8 + 2 * i + t
+            a = half * 8 + 2 * order(i) + t
             f = rowf[:, a].reshape(32, 128)
             lhs[i, t * 128 : (t + 1) * 128, :] = row_operand(f, a).T.astype(BF16)
             s1, s2 = sides(f)
@@ -185,7 +186,7 @@
             gb[i, :, 256 + t * 128 : 256 + (t + 1) * 128] = s2[:80].astype(BF16)
 
     def quarter(i, half, h):
-        a0 = half * 8 + 2 * i
+        a0 = half * 8 + 2 * order(i)
         b0 = (zh if h == 0 else oz) * 4
         e = jnp.exp2(dot(lhs[i], cop[h]))
         ad = jnp.concatenate([jnp.concatenate([adj[a0 + t, b0 + u] for u in range(4)], axis=1) for t in range(2)], axis=0)
@@ -196,7 +197,7 @@
         return dot(jnp.concatenate([wh, wl], axis=1), ctt[h])
 
     def finish_rows(i, half, p):
-        a0 = half * 8 + 2 * i
+        a0 = half * 8 + 2 * order(i)
         for t in range(2):
             q = p[t * 128 : (t + 1) * 128].T
             f = rowf[:, a0 + t].reshape(32, 128)
@@ -206,7 +207,7 @@
             push(rowp.at[lax.rem(y + d, 4), two], yrecv.at[d - 1, two], q_yr.at[a0 // 2], s_yr.at[a0 // 2], ys[d - 1])
 
     def settle(i, half):
-        a0 = half * 8 + 2 * i
+        a0 = half * 8 + 2 * order(i)
         two = pl.ds(a0, 2)
         arrived(yrecv.at[:, two], s_yr.at[a0 // 2])
         ysum[two] = (rowp[y, two] + yrecv[0, two]) + (yrecv[1, two] + yrecv[2, two])
@@ -224,12 +225,10 @@
             def _():
                 push(ysum.at[a], zrecv.at[rho, zl], q_z, s_z, (a, y * 8 + BASE + pi))
 
-    arrived(rowf.at[:, r], s_loc.at[0])
     arrived(rowf.at[:, pl.ds(zh * 8, 7)], s_row)
 
     @pl.when(k == wk)
     def _():
-        arrived(colf.at[:, zh * 4 + x], s_loc.at[1])
         arrived(colf.at[:, pl.ds(0, 3)], s_col)
 
     @pl.when(k != wk)
@@ -247,18 +246,21 @@
     def own_own(i, _):
         row_side(i, zh)
         prow[i] = quarter(i, zh, 0)
-
-        @pl.when(i == 1)
-        def _():
-            arrived(rowf.at[y, pl.ds(oz * 8, 8)], s_far)
-            mine = rowf.at[y, pl.ds(oz * 8, 8)]
-            for d in range(1, 4):
-                push(mine, mine, q_in.at[5], s_yag.at[d - 1], ys[d - 1])
         return 0
 
-    lax.fori_loop(0, 4, own_own, 0)
-
-    pl.semaphore_wait(ready.at[0], 8)
+    lax.fori_loop(0, 4, own_own, 0, unroll=2)
+
+    pl.semaphore_wait(ready.at[0], 11)
+
+    arrived(far, s_far)
+    oth = oz * 8 + x * 2 + k
+    rowf[y, oth] = far[x * 2 + k]
+    spots = [(x * 2 + k, (r, c))] + [(t - zh * 8, to) for to, t in zip(plane, plane_tile, strict=True)]
+    for spot, to in spots:
+        for d in range(4):
+            if spot is not spots[0][0] or d:
+                push(far.at[spot], rowf.at[y, oth], q_in.at[5], s_oth, (to[0], lax.rem(y + d, 4) * 8 + zl))
+
     for to in plane + ys:
         tell(ready.at[1], to)
 
@@ -276,17 +278,16 @@
         finish_rows(i, zh, prow[i] + quarter(i, zh, 1))
         return 0
 
-    lax.fori_loop(0, 4, own_other, 0)
-
-    for d in range(1, 4):
-        arrived(rowf.at[lax.rem(y + 4 - d, 4), pl.ds(oz * 8, 8)], s_yag.at[d - 1])
+    lax.fori_loop(0, 4, own_other, 0, unroll=2)
+
+    arrived(yrecv.reshape(48, 8, 128).at[pl.ds(0, 31)], s_oth)
 
     def other_other(i, _):
         row_side(i, oz)
         prow[i] = quarter(i, oz, 1)
         return 0
 
-    lax.fori_loop(0, 4, other_other, 0)
+    lax.fori_loop(0, 4, other_other, 0, unroll=2)
 
     def col_terms(h):
         half = zh if h == 0 else oz
@@ -343,7 +344,7 @@
         settle(i, zh)
         return 0
 
-    lax.fori_loop(0, 4, other_own, 0)
+    lax.fori_loop(0, 4, other_own, 0, unroll=2)
 
     col_terms(0)
     col_x(0)
@@ -381,22 +382,24 @@
             for z in range(8):
                 t = t + zrecv[q, z]
             fin[q] = -0.5 * t
-        pltpu.make_async_copy(fin, out.at[y, :, place], s_loc.at[4]).start()
-        for d in range(1, 8):
-            push(fin, out.at[y, :, place], q_ag.at[0], s_ag.at[place], dev(zh, x, k, y, lax.rem(zl + d, 8)))
+            zbuf[q, place] = -0.5 * t
+        for d in (5, 3, 4, 2, 6, 1, 7):
+            push(fin, zbuf.at[:, place], q_ag.at[0], s_ag.at[place], dev(zh, x, k, y, lax.rem(zl + d, 8)))
         for d in range(1, 4):
             push(fin, out.at[y, :, place], q_ag.at[1], s_out.at[d - 1], ys[d - 1])
-        arrived(out.at[y, :, place], s_loc.at[4])
 
     for j in range(NP):
         @pl.when(zl != BASE + j)
         def _():
-            arrived(out.at[y, :, j], s_ag.at[j])
+            arrived(zbuf.at[:, j], s_ag.at[j])
             for d in range(1, 4):
-                push(out.at[y, :, j], out.at[y, :, j], q_ag.at[1], s_out.at[d - 1], ys[d - 1])
-
+                push(zbuf.at[:, j], out.at[y, :, j], q_ag.at[1], s_out.at[d - 1], ys[d - 1])
+
+    pltpu.make_async_copy(zbuf, out.at[y], s_loc.at[4]).start()
     for d in range(1, 4):
         arrived(out.at[lax.rem(y + 4 - d, 4)], s_out.at[d - 1])
+
+    arrived(zbuf, s_loc.at[4])
 
     @pl.when(edge)
     def _():
@@ -417,7 +420,7 @@
         for h in range(2):
             arrived(krecv.at[h], q_k.at[h])
     arrived(colf.at[:, pl.ds(0, 7)], q_in.at[3])
-    arrived(rowf.at[pl.ds(0, 3), pl.ds(0, 8)], q_in.at[5])
+    arrived(yrecv.reshape(48, 8, 128).at[pl.ds(0, 31)], q_in.at[5])
     for j in range(8):
         arrived(yrecv.at[:, pl.ds(0, 2)], q_yr.at[j])
 
@@ -451,12 +454,16 @@
     out = pl.pallas_call(
         kernel,
         out_shape=jax.ShapeDtypeStruct((4, NS, NP, 8, 128), F32),
-        in_specs=[pl.BlockSpec(memory_space=pltpu.SMEM), anyspace, anyspace],
+        in_specs=[anyspace] * 3,
         out_specs=anyspace,
         scratch_shapes=[
+            pltpu.SMEM((256,), I32),
             vm((16, 8, 128, 128), BF16),
             vm((4, 16, 8, 128), F32),
+            vm((4, 16, 8, 128), F32),
             vm((4, 8, 8, 128), F32),
+            vm((8, 8, 128), F32),
+            vm((NS, NP, 8, 128), F32),
             vm((2, 256, 512), BF16),
             vm((2, 1024, 128), BF16),
             vm((4, 256, 256), BF16),
@@ -474,7 +481,7 @@
             vm((2, 4, 8, 128), F32),
             vm((NS, 2, 8, 128), F32),
             vm((NS, 8, 128), F32),
-            dma((8,)), dma((5,)), dma, dma, dma, dma, dma, dma((3,)), dma((8,)), dma, dma((2,)), dma((2,)), dma, dma((NP,)), dma((3,)),
+            dma((8,)), dma((5,)), dma, dma, dma, dma, dma, dma, dma((8,)), dma, dma((2,)), dma((2,)), dma, dma((NP,)), dma((3,)),
             dma((6,)), dma((8,)), dma, dma((2,)), dma((2,)), dma, dma((2,)), pltpu.SemaphoreType.REGULAR((2,)),
         ],
         compiler_params=pltpu.CompilerParams(collective_id=0, has_side_effects=True, vmem_limit_bytes=60 << 20),

time: 55.9 us -> 53.4 us (0.955)
  Pallas kernels: 53.9 us -> 50.9 us
    pallas_call x1, Pallas kernels: 53.9 us -> 50.9 us  [per_device(): pl.pallas_call(kernel, out_shape=jax.ShapeDtypeStruct((4, NS, NP, 8, 128)...]
where the time goes in v3:
time: 53.4 us; the launch traced here: 52.6 us
  Pallas kernels  50.9 us (95%)
  local copies, waits for them, and re-layouts  1.67 us (3%)
    pallas_call x1, Pallas kernels, per_device(): pl.pallas_call(kernel, out_shape=jax.ShapeDtypeStruct((4, NS, NP, 8, 128)...  50.9 us
    unnamed x1, local copies, waits for them, and re-layouts  1.67 us

profile of v3, /device:TPU:6, one launch (start us, length us, event | category | flops | bytes accessed | tf_op | source)
XLA Modules:
  0.0 52.6 jit_solution(43378702074923501)
XLA Ops:
  0.0 50.9 %gradient.1 = f32[4,4,4,8,128]{4,3,2,1,0:T(8,128)} custom-call(s32[256]{0:T(256)} %tos_hbm.1, f32[4,16,8,128]{3,2,1,0:T(8,128)} %bitcast.15, bf16[16,8,128,128]{3,2,1,0:T(8,128)(2,1)} %bitcast.14), custom_call_target="tpu_custom_call" | custom-call | flops 5368709120 | bytes 5242880 | tf_op jit(solution)/shard_map/gradient/pallas_call | solution.py:454
  51.0 1.7 %copy.5 = f32[2048,32]{0,1:T(8,128)} copy(f32[2048,32]{0,1:T(8,128)} %bitcast.13) | data formatting | bytes 524288

commit v4 on v3

--- a/solution.py
+++ b/solution.py
@@ -14,7 +14,6 @@
 C1 = 0.25 * math.log2(math.e)
 NP = 4
 NS = 16 // NP
-BASE = (8 - NP) // 2
 FAR = -1e30
 
 
@@ -56,6 +55,10 @@
 
 def dot(a, b):
     return lax.dot_general(a, b, (((1,), (0,)), ((), ())), preferred_element_type=F32)
+
+
+def base(zh):
+    return 1 + zh
 
 
 def dev(zh, x, k, y, zl):
@@ -87,7 +90,7 @@
     oz = 1 - zh
     pi, rho = lax.rem(r, NP), r // NP
     cpi, crho = lax.rem(c16, NP), c16 // NP
-    place = zl - BASE
+    place = zl - base(zh)
     final = (place >= 0) & (place < NP)
     edge = (zl == 0) | (zl == 7)
     plane = [dev(zh, lax.rem(x + d // 2, 4), lax.rem(k + d, 2), y, zl) for d in range(1, 8)]
@@ -213,7 +216,7 @@
         ysum[two] = (rowp[y, two] + yrecv[0, two]) + (yrecv[1, two] + yrecv[2, two])
         for t in range(2):
             a = a0 + t
-            here = (a == r) & (zl == BASE + pi)
+            here = (a == r) & (zl == base(zh) + pi)
 
             @pl.when(here)
             def _():
@@ -223,7 +226,7 @@
 
             @pl.when(jnp.logical_not(here))
             def _():
-                push(ysum.at[a], zrecv.at[rho, zl], q_z, s_z, (a, y * 8 + BASE + pi))
+                push(ysum.at[a], zrecv.at[rho, zl], q_z, s_z, (a, y * 8 + base(half) + pi))
 
     arrived(rowf.at[:, pl.ds(zh * 8, 7)], s_row)
 
@@ -248,7 +251,7 @@
         prow[i] = quarter(i, zh, 0)
         return 0
 
-    lax.fori_loop(0, 4, own_own, 0, unroll=2)
+    lax.fori_loop(0, 4, own_own, 0, unroll=4)
 
     pl.semaphore_wait(ready.at[0], 11)
 
@@ -278,7 +281,7 @@
         finish_rows(i, zh, prow[i] + quarter(i, zh, 1))
         return 0
 
-    lax.fori_loop(0, 4, own_other, 0, unroll=2)
+    lax.fori_loop(0, 4, own_other, 0, unroll=4)
 
     arrived(yrecv.reshape(48, 8, 128).at[pl.ds(0, 31)], s_oth)
 
@@ -287,7 +290,7 @@
         prow[i] = quarter(i, oz, 1)
         return 0
 
-    lax.fori_loop(0, 4, other_other, 0, unroll=2)
+    lax.fori_loop(0, 4, other_other, 0, unroll=4)
 
     def col_terms(h):
         half = zh if h == 0 else oz
@@ -317,8 +320,8 @@
             arrived(xrecv.at[h], s_x.at[h])
             c2[h] = (csum[h, :, x] + xrecv[h, 0]) + (xrecv[h, 1] + xrecv[h, 2])
             for g in range(4):
-                here = (y == g) & (zl == BASE + cpi) if h == 0 else None
-                to = dev(half, x, k, g, BASE + cpi)
+                here = (y == g) & (zl == base(zh) + cpi) if h == 0 else None
+                to = dev(half, x, k, g, base(half) + cpi)
                 if h == 0:
                     @pl.when(here)
                     def _():
@@ -344,7 +347,7 @@
         settle(i, zh)
         return 0
 
-    lax.fori_loop(0, 4, other_own, 0, unroll=2)
+    lax.fori_loop(0, 4, other_own, 0, unroll=4)
 
     col_terms(0)
     col_x(0)
@@ -383,13 +386,15 @@
                 t = t + zrecv[q, z]
             fin[q] = -0.5 * t
             zbuf[q, place] = -0.5 * t
-        for d in (5, 3, 4, 2, 6, 1, 7):
-            push(fin, zbuf.at[:, place], q_ag.at[0], s_ag.at[place], dev(zh, x, k, y, lax.rem(zl + d, 8)))
+        for z in range(8):
+            @pl.when(zl != z)
+            def _():
+                push(fin, zbuf.at[:, place], q_ag.at[0], s_ag.at[place], dev(zh, x, k, y, z))
         for d in range(1, 4):
             push(fin, out.at[y, :, place], q_ag.at[1], s_out.at[d - 1], ys[d - 1])
 
     for j in range(NP):
-        @pl.when(zl != BASE + j)
+        @pl.when(zl != base(zh) + j)
         def _():
             arrived(zbuf.at[:, j], s_ag.at[j])
             for d in range(1, 4):
@@ -424,19 +429,19 @@
     for j in range(8):
         arrived(yrecv.at[:, pl.ds(0, 2)], q_yr.at[j])
 
-    @pl.when(zl == BASE + pi)
+    @pl.when(zl == base(zh) + pi)
     def _():
         arrived(ysum.at[pl.ds(0, 15)], q_z)
 
-    @pl.when(zl != BASE + pi)
+    @pl.when(zl != base(zh) + pi)
     def _():
         arrived(ysum, q_z)
 
-    @pl.when((k == wk) & (zl == BASE + cpi))
+    @pl.when((k == wk) & (zl == base(zh) + cpi))
     def _():
         arrived(c2.reshape(8, 8, 128).at[pl.ds(0, 7)], q_c)
 
-    @pl.when((k == wk) & (zl != BASE + cpi))
+    @pl.when((k == wk) & (zl != base(zh) + cpi))
     def _():
         arrived(c2, q_c)
 

time: 53.4 us -> 52.9 us (level)
  the two profiles are of different devices: /device:TPU:6 before, /device:TPU:4 now
where the time goes in v4:
time: 52.9 us; the launch traced here: 52.7 us
  Pallas kernels  51 us (96%)
  local copies, waits for them, and re-layouts  1.67 us (3%)
    pallas_call x1, Pallas kernels, per_device(): pl.pallas_call(kernel, out_shape=jax.ShapeDtypeStruct((4, NS, NP, 8, 128)...  51 us
    unnamed x1, local copies, waits for them, and re-layouts  1.67 us

profile of v4, /device:TPU:4, one launch (start us, length us, event | category | flops | bytes accessed | tf_op | source)
XLA Modules:
  0.0 52.7 jit_solution(9764826913689968338)
XLA Ops:
  0.0 51.0 %gradient.1 = f32[4,4,4,8,128]{4,3,2,1,0:T(8,128)} custom-call(s32[256]{0:T(256)} %tos_hbm.1, f32[4,16,8,128]{3,2,1,0:T(8,128)} %bitcast.15, bf16[16,8,128,128]{3,2,1,0:T(8,128)(2,1)} %bitcast.14), custom_call_target="tpu_custom_call" | custom-call | flops 5368709120 | bytes 5242880 | tf_op jit(solution)/shard_map/gradient/pallas_call | solution.py:459
  51.0 1.7 %copy.5 = f32[2048,32]{0,1:T(8,128)} copy(f32[2048,32]{0,1:T(8,128)} %bitcast.13) | data formatting | bytes 524288

commit v5 on v4

--- a/solution.py
+++ b/solution.py
@@ -251,7 +251,7 @@
         prow[i] = quarter(i, zh, 0)
         return 0
 
-    lax.fori_loop(0, 4, own_own, 0, unroll=4)
+    lax.fori_loop(0, 2, own_own, 0, unroll=2)
 
     pl.semaphore_wait(ready.at[0], 11)
 
@@ -263,6 +263,8 @@
         for d in range(4):
             if spot is not spots[0][0] or d:
                 push(far.at[spot], rowf.at[y, oth], q_in.at[5], s_oth, (to[0], lax.rem(y + d, 4) * 8 + zl))
+
+    lax.fori_loop(2, 4, own_own, 0, unroll=2)
 
     for to in plane + ys:
         tell(ready.at[1], to)

time: 52.9 us -> 52.1 us (0.985)
  Pallas kernels: 51 us -> 50.3 us
    pallas_call x1, Pallas kernels: 51 us -> 50.3 us  [per_device(): pl.pallas_call(kernel, out_shape=jax.ShapeDtypeStruct((4, NS, NP, 8, 128)...]
where the time goes in v5:
time: 52.1 us; the launch traced here: 52 us
  Pallas kernels  50.3 us (97%)
  local copies, waits for them, and re-layouts  1.67 us (3%)
    pallas_call x1, Pallas kernels, per_device(): pl.pallas_call(kernel, out_shape=jax.ShapeDtypeStruct((4, NS, NP, 8, 128)...  50.3 us
    unnamed x1, local copies, waits for them, and re-layouts  1.67 us

profile of v5, /device:TPU:4, one launch (start us, length us, event | category | flops | bytes accessed | tf_op | source)
XLA Modules:
  0.0 52.0 jit_solution(4829747797279032013)
XLA Ops:
  0.0 50.3 %gradient.1 = f32[4,4,4,8,128]{4,3,2,1,0:T(8,128)} custom-call(s32[256]{0:T(256)} %tos_hbm.1, f32[4,16,8,128]{3,2,1,0:T(8,128)} %bitcast.15, bf16[16,8,128,128]{3,2,1,0:T(8,128)(2,1)} %bitcast.14), custom_call_target="tpu_custom_call" | custom-call | flops 5368709120 | bytes 5242880 | tf_op jit(solution)/shard_map/gradient/pallas_call | solution.py:461
  50.3 1.7 %copy.5 = f32[2048,32]{0,1:T(8,128)} copy(f32[2048,32]{0,1:T(8,128)} %bitcast.13) | data formatting | bytes 524288
